TPU v7x, 32 devices: a whole 2x2x4 slice. The times are simulated.
32 devices in a mesh: ctx: 8 (over z, core), tp: 4 (over y, x).
Axes of the slice: x: 2, y: 2, z: 4, core: 2. Of those that a mesh axis runs over, the one named last changes fastest.
Arguments:
- query_latent: bfloat16 [4096, 64, 512], P('ctx', 'tp'), may hold values from -24 to 24
- query_rope: bfloat16 [4096, 4096], P('ctx', 'tp'), may hold values from -24 to 24
- key_latent: bfloat16 [4096, 512], P('ctx'), may hold values from -6 to 6
- key_rope: bfloat16 [2048, 128], P('ctx'), may hold values from -6 to 6
- block_ids: int32 [16], replicated, may hold values from 0 to 15, as said below
- value_up: bfloat16 [64, 512, 128], P('tp'), may hold values from -0.5 to 0.5
- out_weight: bfloat16 [8192, 7168], P('tp'), may hold values from -0.0625 to 0.0625
- residual: bfloat16 [4096, 7168], P(('ctx', 'tp')), may hold values from -18 to 18
- norm_gain: float32 [7168], replicated, may hold values from 0.1 to 1.9
- gate_weight: bfloat16 [7168, 2048], P('ctx', 'tp'), may hold values from -0.0625 to 0.0625
- up_weight: bfloat16 [7168, 2048], P('ctx', 'tp'), may hold values from -0.0625 to 0.0625
- down_weight: bfloat16 [7168, 2048], P('ctx', 'tp'), may hold values from -0.125 to 0.125
Outputs:
- layer_out: bfloat16 [4096, 7168], P(('ctx', 'tp'))
Inputs may be any that keep to these rules, and one draw needn't show every extreme that they name: `block_ids`: index c of ctx stores blocks 2c and 2c + 1; their two entries sum to 15, and every value appears once.
All inputs are finite; a program needn't handle non-finite values.
Results may differ from a plain program's by a relative error of at most 0.018.
Values may be sent and summed in bfloat16 or wider, within the bound.
A program may use at most 192 MiB of HBM per device.

v0:
```python
import jax
import jax.numpy as jnp
from jax import lax
from jax.sharding import PartitionSpec as P


def from_behind(x, axis, by):
    length = lax.axis_size(axis)
    return lax.ppermute(x, axis, [(i, (i + by) % length) for i in range(length)])


def rms_norm(activation, gain_vector):
    mean_square = jnp.mean(activation * activation, axis=-1, keepdims=True)
    return (activation * lax.rsqrt(mean_square + 1e-06) * gain_vector).astype(jnp.bfloat16)


def local(
    query_latent,
    query_rope,
    key_latent,
    key_rope,
    block_ids,
    value_up,
    out_weight,
    residual,
    norm_gain,
    gate_weight,
    up_weight,
    down_weight,
):
    seq_rows = key_latent.shape[0]
    half_len = seq_rows // 2
    head_count = query_latent.shape[1]
    rope_dim = key_rope.shape[1] // 2
    head_dim = value_up.shape[2]
    ctx_count = lax.axis_size("ctx")
    tp_count = lax.axis_size("tp")
    score_scale = (head_dim + rope_dim) ** (-0.5)
    recv_latent, recv_rope = from_behind((key_latent, key_rope), "ctx", 1)
    keys_lat = jnp.concatenate([key_latent, recv_latent], axis=0)
    keys_rot = jnp.concatenate(
        [key_rope.reshape(seq_rows, rope_dim), recv_rope.reshape(seq_rows, rope_dim)], axis=0
    )
    current = lax.axis_index("ctx")
    previous = (current + ctx_count - 1) % ctx_count
    own_ids = lax.dynamic_slice_in_dim(block_ids, current * 2, 2, 0)
    prev_ids = lax.dynamic_slice_in_dim(block_ids, previous * 2, 2, 0)
    row_index = jnp.arange(seq_rows, dtype=jnp.int32)
    first_half = row_index < half_len
    offset = row_index % half_len
    query_pos = jnp.where(first_half, own_ids[0], own_ids[1]) * half_len + offset
    key_pos = jnp.concatenate(
        [query_pos, jnp.where(first_half, prev_ids[0], prev_ids[1]) * half_len + offset], axis=0
    )
    rope_queries = query_rope.reshape(seq_rows, head_count, rope_dim)
    block_rows = min(seq_rows, 512)

    def attend(block_index):
        scores = jnp.einsum(
            "shl,kl->hsk", query_latent, keys_lat, preferred_element_type=jnp.float32
        )
        scores = scores + jnp.einsum(
            "shr,kr->hsk", rope_queries, keys_rot, preferred_element_type=jnp.float32
        )
        scores = scores * score_scale
        visible = key_pos[None, :] <= query_pos[:, None]
        scores = jnp.where(visible[None], scores, -jnp.inf)
        highest = jnp.max(scores, axis=-1, keepdims=True)
        exponent = jnp.exp(scores - highest)
        weights = (exponent / jnp.sum(exponent, axis=-1, keepdims=True)).astype(jnp.bfloat16)
        blended = jnp.einsum(
            "hsk,kl->shl", weights, keys_lat, preferred_element_type=jnp.float32
        ).astype(jnp.bfloat16)
        values = jnp.einsum(
            "shl,hlv->shv", blended, value_up, preferred_element_type=jnp.float32
        ).astype(jnp.bfloat16)
        return values.reshape(block_rows, head_count * head_dim)

    head_out = lax.map(attend, jnp.arange(seq_rows // block_rows, dtype=jnp.int32)).reshape(
        seq_rows, head_count * head_dim
    )
    share_rows = seq_rows // tp_count
    tp_index = lax.axis_index("tp")
    partial_attn = jnp.dot(head_out, out_weight, preferred_element_type=jnp.float32)
    attn_total = lax.psum(partial_attn.astype(jnp.bfloat16), "tp").astype(jnp.float32)
    all_residual = lax.all_gather(residual, "tp", axis=0, tiled=True)
    hidden_state = all_residual.astype(jnp.float32) + attn_total
    normed_all = rms_norm(hidden_state, norm_gain)
    own_state = lax.dynamic_slice_in_dim(hidden_state, tp_index * share_rows, share_rows, 0)
    gate_full, up_full, down_full = (
        lax.all_gather(gate_weight, "ctx", axis=0, tiled=True),
        lax.all_gather(up_weight, "ctx", axis=0, tiled=True),
        lax.all_gather(down_weight, "ctx", axis=0, tiled=True),
    )
    gate_proj = jnp.dot(normed_all, gate_full, preferred_element_type=jnp.float32)
    up_proj = jnp.dot(normed_all, up_full, preferred_element_type=jnp.float32)
    hidden_units = (jax.nn.silu(gate_proj) * up_proj).astype(jnp.bfloat16)
    shared_part = lax.psum_scatter(
        lax.dot_general(
            hidden_units, down_full, (((1,), (1,)), ((), ())), preferred_element_type=jnp.float32
        ).astype(jnp.bfloat16),
        "tp",
        scatter_dimension=0,
        tiled=True,
    ).astype(jnp.float32)
    return (own_state + shared_part).astype(jnp.bfloat16)


def solution(mesh):
    placed = (
        P("ctx", "tp", None),
        P("ctx", "tp"),
        P("ctx", None),
        P("ctx", None),
        P(),
        P("tp", None, None),
        P("tp", None),
        P(("ctx", "tp"), None),
        P(),
        P("ctx", "tp"),
        P("ctx", "tp"),
        P("ctx", "tp"),
    )
    return jax.shard_map(
        local, mesh=mesh, in_specs=placed, out_specs=P(("ctx", "tp"), None), check_vma=False
    )
```

profile of v0, /device:TPU:0, one launch (start us, length us, event | category | flops | bytes accessed | tf_op | source)
XLA Modules:
  0.0 672.1 jit_solution(7638917272089841626)
XLA Ops:
  6.5 0.0 copy-start
  6.5 0.0 all-reduce.2.cloned.1.call-start
  6.5 0.5 collective-permute-start
  7.0 2.7 collective-permute-start.1
  9.7 0.8 fusion.35
  10.5 0.6 fusion.34
  11.1 1.2 fusion.22
  12.3 1.3 multiply_add_fusion
  13.6 1.2 broadcast_compare_fusion
  14.8 0.9 reshape.69
  15.7 1.5 copy.19
  17.2 0.1 copy.17
  17.3 1.5 collective-permute-done.1
  18.8 0.1 reshape.70
  18.9 0.1 copy.18
  19.0 0.0 collective-permute-done
  19.0 18.1 %fusion.3 = f32[1024,512,16]{1,0,2:T(8,128)} fusion(bf16[512,16,512]{2,1,0:T(8,128)(2,1)} %param.12, bf16[512,512]{1,0:T(8,128)(2,1)} %collective-permute-done, bf16[512,512]{1,0:T(8,128)(2,1)} %param.14), kind=kOutput, calls=%fused_computation.11 | convolution fusion | flops 8592031744 | bytes 42991616 | tf_op jit(solution)/shard_map/while/body/eval_jaxpr/shl,kl->hsk/dot_general | solution.py:59
  37.1 24.3 %fusion.37 = (f32[16,512]{1,0:T(8,128)S(1)}, f32[16,512,1024]{1,2,0:T(8,128)}) fusion(f32[1024,512,16]{1,0,2:T(8,128)} %fusion.3, pred[512,1024]{0,1:T(8,128)(4,1)} %broadcast_compare_fusion, bf16[512,16,64]{0,2,1:T(8,128)(2,1)S(1)} %bitcast.36, bf16[512,64]{0,1:T(8,128)(2,1)S(1)} %copy.18, bf16[512,64]{0,1:T(8,128)(2,1)S(1)} %copy.17), kind=kOutput, calls=%fused_computation.51 | convolution fusion | flops 1115948032 | bytes 68845568 | tf_op jit(solution)/shard_map/while/body/eval_jaxpr/sub | solution.py:69
  61.3 0.0 copy-done
  61.3 17.5 %fusion.9 = bf16[16,512,128]{1,2,0:T(8,128)(2,1)} fusion(bf16[16,512,128]{2,1,0:T(8,128)(2,1)S(1)} %copy-done, f32[16,512,1024]{1,2,0:T(8,128)} %get-tuple-element.41, f32[16,512]{1,0:T(8,128)S(1)} %get-tuple-element.40, bf16[512,512]{1,0:T(8,128)(2,1)} %collective-permute-done, bf16[512,512]{1,0:T(8,128)(2,1)} %param.14), kind=kOutput, calls=%fused_computation.17 | convolution fusion | flops 9687793664 | bytes 38830080 | tf_op jit(solution)/shard_map/while/body/eval_jaxpr/shl,hlv->shv/dot_general | solution.py:74
  78.9 23.3 %convolution_convert_fusion.1 = bf16[512,7168]{1,0:T(8,128)(2,1)} fusion(bf16[512,2048]{0,1:T(8,128)(2,1)} %bitcast.37, bf16[2048,7168]{1,0:T(8,128)(2,1)} %param.18), kind=kOutput, calls=%fused_computation.10 | convolution fusion | flops 15036055552 | bytes 38797312 | tf_op jit(solution)/shard_map/dot_general | solution.py:84
  102.2 0.0 all-reduce.2.cloned.1.call-update
  102.2 0.0 all-gather.5.cloned.1.call-start
  102.3 0.7 all-gather.5.cloned.1.call-update
  103.0 0.0 all-gather.7.cloned.1.call-start
  103.0 0.7 all-gather.7.cloned.1.call-update
  103.7 0.0 all-gather.11.cloned.1.call-start
  103.7 0.5 all-gather.11.cloned.1.call-update
  104.3 0.0 all-gather.9.cloned.1.call-start
  104.3 0.5 all-gather.9.cloned.1.call-update
  104.9 0.0 copy-start.2
  104.9 0.0 reduce-scatter.2.cloned.1.call-start
  104.9 153.2 %all-reduce.2.cloned.1.call-done = bf16[512,7168]{1,0:T(8,128)(2,1)} async-done(((bf16[512,7168]{1,0:T(8,128)(2,1)}), bf16[512,7168]{1,0:T(8,128)(2,1)}) %all-reduce.2.cloned.1.call-update) | async-done | bytes 7340048 | tf_op jit(solution)/shard_map/psum | solution.py:85
  258.1 80.8 %all-gather.5.cloned.1.call-done = bf16[512,7168]{1,0:T(8,128)(2,1)} async-done(((bf16[128,7168]{1,0:T(8,128)(2,1)}), bf16[512,7168]{1,0:T(8,128)(2,1)}) %all-gather.5.cloned.1.call-update) | async-done | bytes 7340048 | tf_op jit(solution)/shard_map/all_gather | solution.py:86
  338.9 13.5 %convert_add_fusion = (f32[512,7168]{1,0:T(8,128)}, f32[512]{0:T(512)S(1)}) fusion(bf16[512,7168]{1,0:T(8,128)(2,1)} %all-reduce.2.cloned.1.call-done, bf16[512,7168]{1,0:T(8,128)(2,1)} %all-gather.5.cloned.1.call-done), kind=kLoop, calls=%fused_computation.7 | loop fusion | flops 18349568 | bytes 29362176 | tf_op jit(solution)/shard_map/add | solution.py:87
  352.4 61.6 %all-gather.7.cloned.1.call-done = bf16[7168,512]{1,0:T(8,128)(2,1)} async-done(((bf16[896,512]{1,0:T(8,128)(2,1)}), bf16[7168,512]{1,0:T(8,128)(2,1)}) %all-gather.7.cloned.1.call-update) | async-done | bytes 7340048 | tf_op jit(solution)/shard_map/all_gather | solution.py:91
  413.9 0.0 copy-done.2
  413.9 9.7 %fusion.33 = f32[512,512]{1,0:T(8,128)S(1)} fusion(bf16[7168,512]{1,0:T(8,128)(2,1)} %all-gather.7.cloned.1.call-done, f32[7168]{0:T(1024)S(1)} %copy-done.2, f32[512]{0:T(512)S(1)} %add_rsqrt_fusion, bf16[512,7168]{1,0:T(8,128)(2,1)} %all-reduce.2.cloned.1.call-done, bf16[512,7168]{1,0:T(8,128)(2,1)} %all-gather.5.cloned.1.call-done), kind=kOutput, calls=%fused_computation.47 | convolution fusion | flops 3780116480 | bytes 23099392 | tf_op jit(solution)/shard_map/dot_general | solution.py:95
  423.7 63.8 %all-gather.11.cloned.1.call-done = bf16[7168,512]{1,0:T(8,128)(2,1)} async-done(((bf16[896,512]{1,0:T(8,128)(2,1)}), bf16[7168,512]{1,0:T(8,128)(2,1)}) %all-gather.11.cloned.1.call-update) | async-done | bytes 7340048 | tf_op jit(solution)/shard_map/all_gather | solution.py:93
  487.5 73.5 %all-gather.9.cloned.1.call-done = bf16[7168,512]{1,0:T(8,128)(2,1)} async-done(((bf16[896,512]{1,0:T(8,128)(2,1)}), bf16[7168,512]{1,0:T(8,128)(2,1)}) %all-gather.9.cloned.1.call-update) | async-done | bytes 7340048 | tf_op jit(solution)/shard_map/all_gather | solution.py:92
  561.0 22.3 %convolution_convert_fusion = bf16[512,7168]{1,0:T(8,128)(2,1)} fusion(bf16[7168,512]{1,0:T(8,128)(2,1)} %all-gather.11.cloned.1.call-done, bf16[7168,512]{1,0:T(8,128)(2,1)} %all-gather.9.cloned.1.call-done, f32[512,512]{1,0:T(8,128)S(1)} %fusion.33, f32[7168]{0:T(1024)S(1)} %copy-done.2, f32[512]{0:T(512)S(1)} %add_rsqrt_fusion, ...), kind=kOutput, calls=%fused_computation.9 | convolution fusion | flops 7543455744 | bytes 37779456 | tf_op jit(solution)/shard_map/dot_general | solution.py:99
  583.3 0.0 copy-start.1
  583.3 0.0 reduce-scatter.2.cloned.1.call-update
  583.3 77.7 %reduce-scatter.2.cloned.1.call-done = bf16[128,7168]{1,0:T(8,128)(2,1)} async-done(((bf16[512,7168]{1,0:T(8,128)(2,1)}), bf16[128,7168]{1,0:T(8,128)(2,1)}) %reduce-scatter.2.cloned.1.call-update) | async-done | bytes 1835024 | tf_op jit(solution)/shard_map/reduce_scatter | solution.py:98
  661.1 4.2 add_convert_fusion
  665.2 0.0 copy-done.1
  (2 shorter events, 0.0 us)
Async XLA Ops:
  6.5 54.8 %copy-start = (bf16[16,512,128]{2,1,0:T(8,128)(2,1)S(1)}, bf16[16,512,128]{2,1,0:T(8,128)(2,1)}, u32[]{:S(2)}) copy-start(bf16[16,512,128]{2,1,0:T(8,128)(2,1)} %param.17) | copy-start | bytes 6291460
  6.5 251.6 %all-reduce.2.cloned.1.call-start = ((), (), s32[]{:S(2)}) async-start(), calls=%async_computation.2 | async-start | bytes 14680064 | tf_op jit(solution)/shard_map/psum | solution.py:85
  6.5 12.5 %collective-permute-start = (bf16[512,512]{1,0:T(8,128)(2,1)}, bf16[512,512]{1,0:T(8,128)(2,1)}, u32[]{:S(2)}, u32[]{:S(2)}) collective-permute-start(bf16[512,512]{1,0:T(8,128)(2,1)} %param.14), channel_id=1, source_target_pairs={{0,4},{4,8},{8,12},{12,16},{16,20},{20,24},{24,28},{28,0},{1,5},{5... | collective-permute-start | bytes 1572872 | tf_op jit(solution)/shard_map/ppermute | solution.py:9
  7.0 11.8 %collective-permute-start.1 = (bf16[256,128]{1,0:T(8,128)(2,1)}, bf16[256,128]{1,0:T(8,128)(2,1)S(1)}, u32[]{:S(2)}, u32[]{:S(2)}) collective-permute-start(bf16[256,128]{1,0:T(8,128)(2,1)} %param.15), channel_id=1, source_target_pairs={{0,4},{4,8},{8,12},{12,16},{16,20},{20,24},{24,28},{28,0},{1,5},{5... | collective-permute-start | bytes 196616 | tf_op jit(solution)/shard_map/ppermute | solution.py:9
  102.2 236.6 %all-gather.5.cloned.1.call-start = ((), (), s32[]{:S(2)}) async-start(), calls=%async_computation.1 | async-start | bytes 9175040 | tf_op jit(solution)/shard_map/all_gather | solution.py:86
  103.0 311.0 %all-gather.7.cloned.1.call-start = ((), (), s32[]{:S(2)}) async-start(), calls=%async_computation.3 | async-start | bytes 8257536 | tf_op jit(solution)/shard_map/all_gather | solution.py:91
  103.7 383.8 %all-gather.11.cloned.1.call-start = ((), (), s32[]{:S(2)}) async-start(), calls=%async_computation.5 | async-start | bytes 8257536 | tf_op jit(solution)/shard_map/all_gather | solution.py:93
  104.3 456.7 %all-gather.9.cloned.1.call-start = ((), (), s32[]{:S(2)}) async-start(), calls=%async_computation.4 | async-start | bytes 8257536 | tf_op jit(solution)/shard_map/all_gather | solution.py:92
  104.9 309.1 %copy-start.2 = (f32[7168]{0:T(1024)S(1)}, f32[7168]{0:T(1024)}, u32[]{:S(2)}) copy-start(f32[7168]{0:T(1024)} %param.20) | copy-start | bytes 86020
  104.9 556.2 %reduce-scatter.2.cloned.1.call-start = ((), (), s32[]{:S(2)}) async-start(), calls=%async_computation.6 | async-start | bytes 9175040 | tf_op jit(solution)/shard_map/reduce_scatter | solution.py:98
  583.3 81.9 %copy-start.1 = (bf16[16,512,128]{2,1,0:T(8,128)(2,1)S(1)}, bf16[16,512,128]{2,1,0:T(8,128)(2,1)}, u32[]{:S(2)}) copy-start(bf16[16,512,128]{2,1,0:T(8,128)(2,1)} %param.17) | copy-start | bytes 6291460
Sparse Core Ops, SparseCore 0:
  102.3 155.7 all-reduce.1
  259.9 78.8 all-gather.4
  340.5 73.3 all-gather.6
  415.4 71.9 all-gather.10
  489.0 71.9 all-gather.8
  583.5 77.5 reduce-scatter.1
where the time goes:
time: 672 us
  waiting for transfers between devices  515 us (77%)
  matrix products  115 us (17%)
  other arithmetic  21.3 us (3%)
  between operations  13.6 us (2%)
    psum x1, waiting for transfers between devices, local(): lax.psum(partial_attn.astype(jnp.bfloat16), 'tp').astype(jnp.float32)  153 us
    all_gather x1, waiting for transfers between devices, local(): all_residual = lax.all_gather(residual, 'tp', axis=0, tiled=True)  80.8 us
    reduce_scatter x1, waiting for transfers between devices, local(): lax.psum_scatter(lax.dot_general(hidden_units, down_full, (((1,), (1,)),...  77.7 us
    all_gather x1, waiting for transfers between devices, local(): lax.all_gather(up_weight, 'ctx', axis=0, tiled=True)  73.5 us
    all_gather x1, waiting for transfers between devices, local(): lax.all_gather(down_weight, 'ctx', axis=0, tiled=True)  63.8 us
    all_gather x1, waiting for transfers between devices, local(): lax.all_gather(gate_weight, 'ctx', axis=0, tiled=True)  61.6 us
    sub x1, matrix products, attend(): exponent = jnp.exp(scores - highest)  24.3 us
    dot_general x1, matrix products, local(): jnp.dot(head_out, out_weight, preferred_element_type=jnp.float32)  23.3 us
  transfers between devices with their start and end apart: 8, of which 7 were waited for; matrix products, arithmetic and copies ran while one was open for 5% of the time, Pallas kernels for 0%

commit v1 on v0

--- a/solution.py
+++ b/solution.py
@@ -2,6 +2,8 @@
 import jax.numpy as jnp
 from jax import lax
 from jax.sharding import PartitionSpec as P
+
+blocks_list = lambda sheet, peer_axis: jnp.sum(jax.lax.all_gather(sheet, peer_axis), axis=0)
 
 
 def from_behind(x, axis, by):
@@ -82,7 +84,7 @@
     share_rows = seq_rows // tp_count
     tp_index = lax.axis_index("tp")
     partial_attn = jnp.dot(head_out, out_weight, preferred_element_type=jnp.float32)
-    attn_total = lax.psum(partial_attn.astype(jnp.bfloat16), "tp").astype(jnp.float32)
+    attn_total = blocks_list(partial_attn.astype(jnp.bfloat16), "tp").astype(jnp.float32)
     all_residual = lax.all_gather(residual, "tp", axis=0, tiled=True)
     hidden_state = all_residual.astype(jnp.float32) + attn_total
     normed_all = rms_norm(hidden_state, norm_gain)

time: 672 us -> 779 us (1.16)
  waiting for transfers between devices: 515 us -> 605 us
  other arithmetic: 21.3 us -> 37.5 us
    all_gather x0 -> x1, waiting for transfers between devices: none -> 260 us  [jax.lax.all_gather(sheet, peer_axis)]
    psum x1 -> x0, waiting for transfers between devices: 153 us -> none  [local(): lax.psum(partial_attn.astype(jnp.bfloat16), 'tp').astype(jnp.float32)]
    all_gather x1, waiting for transfers between devices: 80.8 us -> 64.6 us  [local(): all_residual = lax.all_gather(residual, 'tp', axis=0, tiled=True)]
    reduce_sum x0 -> x1, other arithmetic: none -> 16.2 us  [jnp.sum(jax.lax.all_gather(sheet, peer_axis), axis=0)]
    all_gather x1, waiting for transfers between devices: 63.8 us -> 73.5 us  [local(): lax.all_gather(down_weight, 'ctx', axis=0, tiled=True)]
    all_gather x1, waiting for transfers between devices: 73.5 us -> 63.8 us  [local(): lax.all_gather(up_weight, 'ctx', axis=0, tiled=True)]
  transfers between devices with their start and end apart: 8 -> 8, of which waited for: 7 -> 7; matrix products, arithmetic and copies ran while one was open for 5% -> 6% of each run, Pallas kernels for 0% -> 0%
where the time goes in v1:
time: 779 us
  waiting for transfers between devices  605 us (78%)
  matrix products  115 us (15%)
  other arithmetic  37.5 us (5%)
  between operations  13.6 us (2%)
    all_gather x1, waiting for transfers between devices, jax.lax.all_gather(sheet, peer_axis)  260 us
    reduce_scatter x1, waiting for transfers between devices, local(): lax.psum_scatter(lax.dot_general(hidden_units, down_full, (((1,), (1,)),...  77.8 us
    all_gather x1, waiting for transfers between devices, local(): lax.all_gather(down_weight, 'ctx', axis=0, tiled=True)  73.5 us
    all_gather x1, waiting for transfers between devices, local(): all_residual = lax.all_gather(residual, 'tp', axis=0, tiled=True)  64.6 us
    all_gather x1, waiting for transfers between devices, local(): lax.all_gather(up_weight, 'ctx', axis=0, tiled=True)  63.8 us
    all_gather x1, waiting for transfers between devices, local(): lax.all_gather(gate_weight, 'ctx', axis=0, tiled=True)  61.6 us
    sub x1, matrix products, attend(): exponent = jnp.exp(scores - highest)  24.3 us
    dot_general x1, matrix products, local(): jnp.dot(head_out, out_weight, preferred_element_type=jnp.float32)  23.3 us
  transfers between devices with their start and end apart: 8, of which 7 were waited for; matrix products, arithmetic and copies ran while one was open for 6% of the time, Pallas kernels for 0%

profile of v1, /device:TPU:0, one launch (start us, length us, event | category | flops | bytes accessed | tf_op | source)
XLA Modules:
  0.0 778.6 jit_solution(14536248824211629392)
XLA Ops:
  6.5 0.0 copy-start
  6.5 0.0 all-gather.15.cloned.1.call-start
  6.5 0.5 collective-permute-start
  7.0 2.7 collective-permute-start.1
  9.7 0.8 fusion.35
  10.5 0.6 fusion.34
  11.1 1.2 fusion.22
  12.3 1.3 multiply_add_fusion
  13.6 1.2 broadcast_compare_fusion
  14.8 0.9 reshape.69
  15.7 1.5 copy.19
  17.2 0.1 copy.17
  17.3 1.5 collective-permute-done.1
  18.8 0.1 reshape.70
  18.9 0.1 copy.18
  19.0 0.0 collective-permute-done
  19.0 18.1 %fusion.3 = f32[1024,512,16]{1,0,2:T(8,128)} fusion(bf16[512,16,512]{2,1,0:T(8,128)(2,1)} %param.12, bf16[512,512]{1,0:T(8,128)(2,1)} %collective-permute-done, bf16[512,512]{1,0:T(8,128)(2,1)} %param.14), kind=kOutput, calls=%fused_computation.11 | convolution fusion | flops 8592031744 | bytes 42991616 | tf_op jit(solution)/shard_map/while/body/eval_jaxpr/shl,kl->hsk/dot_general | solution.py:61
  37.1 24.3 %fusion.37 = (f32[16,512]{1,0:T(8,128)S(1)}, f32[16,512,1024]{1,2,0:T(8,128)}) fusion(f32[1024,512,16]{1,0,2:T(8,128)} %fusion.3, pred[512,1024]{0,1:T(8,128)(4,1)} %broadcast_compare_fusion, bf16[512,16,64]{0,2,1:T(8,128)(2,1)S(1)} %bitcast.38, bf16[512,64]{0,1:T(8,128)(2,1)S(1)} %copy.18, bf16[512,64]{0,1:T(8,128)(2,1)S(1)} %copy.17), kind=kOutput, calls=%fused_computation.51 | convolution fusion | flops 1115948032 | bytes 68845568 | tf_op jit(solution)/shard_map/while/body/eval_jaxpr/sub | solution.py:71
  61.3 0.0 copy-done
  61.3 17.5 %fusion.9 = bf16[16,512,128]{1,2,0:T(8,128)(2,1)} fusion(bf16[16,512,128]{2,1,0:T(8,128)(2,1)S(1)} %copy-done, f32[16,512,1024]{1,2,0:T(8,128)} %get-tuple-element.41, f32[16,512]{1,0:T(8,128)S(1)} %get-tuple-element.40, bf16[512,512]{1,0:T(8,128)(2,1)} %collective-permute-done, bf16[512,512]{1,0:T(8,128)(2,1)} %param.14), kind=kOutput, calls=%fused_computation.17 | convolution fusion | flops 9687793664 | bytes 38830080 | tf_op jit(solution)/shard_map/while/body/eval_jaxpr/shl,hlv->shv/dot_general | solution.py:76
  78.9 23.3 %convolution_convert_fusion.1 = bf16[512,7168]{1,0:T(8,128)(2,1)} fusion(bf16[512,2048]{0,1:T(8,128)(2,1)} %bitcast.39, bf16[2048,7168]{1,0:T(8,128)(2,1)} %param.18), kind=kOutput, calls=%fused_computation.10 | convolution fusion | flops 15036055552 | bytes 38797312 | tf_op jit(solution)/shard_map/dot_general | solution.py:86
  102.2 0.0 all-gather.15.cloned.1.call-update
  102.2 0.0 all-gather.7.cloned.1.call-start
  102.3 0.7 all-gather.7.cloned.1.call-update
  103.0 0.0 all-gather.9.cloned.1.call-start
  103.0 0.7 all-gather.9.cloned.1.call-update
  103.7 0.0 all-gather.11.cloned.1.call-start
  103.7 0.5 all-gather.11.cloned.1.call-update
  104.3 0.0 all-gather.13.cloned.1.call-start
  104.3 0.5 all-gather.13.cloned.1.call-update
  104.9 0.0 reduce-scatter.2.cloned.1.call-start
  104.9 259.7 %all-gather.15.cloned.1.call-done = bf16[2048,7168]{1,0:T(8,128)(2,1)} async-done(((bf16[512,7168]{1,0:T(8,128)(2,1)}), bf16[2048,7168]{1,0:T(8,128)(2,1)}) %all-gather.15.cloned.1.call-update) | async-done | bytes 29360144 | tf_op jit(solution)/shard_map/all_gather | solution.py:6
  364.6 16.2 %reduce_sum.32 = bf16[512,7168]{1,0:T(8,128)(2,1)} reduce(bf16[4,512,7168]{2,1,0:T(8,128)(2,1)} %bitcast.37, bf16[]{:T(256)} %constant.73.clone.1), dimensions={0}, to_apply=%region_2.3 | reduce | flops 11010048 | bytes 36700160 | tf_op jit(solution)/shard_map/reduce_sum | solution.py:6
  380.8 0.0 copy-start.2
  380.8 64.6 %all-gather.7.cloned.1.call-done = bf16[512,7168]{1,0:T(8,128)(2,1)} async-done(((bf16[128,7168]{1,0:T(8,128)(2,1)}), bf16[512,7168]{1,0:T(8,128)(2,1)}) %all-gather.7.cloned.1.call-update) | async-done | bytes 7340048 | tf_op jit(solution)/shard_map/all_gather | solution.py:88
  445.4 13.5 %convert_add_fusion = (f32[512,7168]{1,0:T(8,128)}, f32[512]{0:T(512)S(1)}) fusion(bf16[512,7168]{1,0:T(8,128)(2,1)} %reduce_sum.32, bf16[512,7168]{1,0:T(8,128)(2,1)} %all-gather.7.cloned.1.call-done), kind=kLoop, calls=%fused_computation.7 | loop fusion | flops 18349568 | bytes 29362176 | tf_op jit(solution)/shard_map/add | solution.py:89
  458.9 61.6 %all-gather.9.cloned.1.call-done = bf16[7168,512]{1,0:T(8,128)(2,1)} async-done(((bf16[896,512]{1,0:T(8,128)(2,1)}), bf16[7168,512]{1,0:T(8,128)(2,1)}) %all-gather.9.cloned.1.call-update) | async-done | bytes 7340048 | tf_op jit(solution)/shard_map/all_gather | solution.py:93
  520.5 0.0 copy-done.2
  520.5 9.7 %fusion.33 = f32[512,512]{1,0:T(8,128)S(1)} fusion(bf16[7168,512]{1,0:T(8,128)(2,1)} %all-gather.9.cloned.1.call-done, f32[7168]{0:T(1024)S(1)} %copy-done.2, f32[512]{0:T(512)S(1)} %add_rsqrt_fusion, bf16[512,7168]{1,0:T(8,128)(2,1)} %reduce_sum.32, bf16[512,7168]{1,0:T(8,128)(2,1)} %all-gather.7.cloned.1.call-done), kind=kOutput, calls=%fused_computation.47 | convolution fusion | flops 3780116480 | bytes 23099392 | tf_op jit(solution)/shard_map/dot_general | solution.py:97
  530.2 63.8 %all-gather.11.cloned.1.call-done = bf16[7168,512]{1,0:T(8,128)(2,1)} async-done(((bf16[896,512]{1,0:T(8,128)(2,1)}), bf16[7168,512]{1,0:T(8,128)(2,1)}) %all-gather.11.cloned.1.call-update) | async-done | bytes 7340048 | tf_op jit(solution)/shard_map/all_gather | solution.py:94
  594.0 73.5 %all-gather.13.cloned.1.call-done = bf16[7168,512]{1,0:T(8,128)(2,1)} async-done(((bf16[896,512]{1,0:T(8,128)(2,1)}), bf16[7168,512]{1,0:T(8,128)(2,1)}) %all-gather.13.cloned.1.call-update) | async-done | bytes 7340048 | tf_op jit(solution)/shard_map/all_gather | solution.py:95
  667.5 22.3 %convolution_convert_fusion = bf16[512,7168]{1,0:T(8,128)(2,1)} fusion(bf16[7168,512]{1,0:T(8,128)(2,1)} %all-gather.13.cloned.1.call-done, bf16[7168,512]{1,0:T(8,128)(2,1)} %all-gather.11.cloned.1.call-done, f32[512,512]{1,0:T(8,128)S(1)} %fusion.33, f32[7168]{0:T(1024)S(1)} %copy-done.2, f32[512]{0:T(512)S(1)} %add_rsqrt_fusion, ...), kind=kOutput, calls=%fused_computation.9 | convolution fusion | flops 7543455744 | bytes 37779456 | tf_op jit(solution)/shard_map/dot_general | solution.py:101
  689.8 0.0 copy-start.1
  689.8 0.0 reduce-scatter.2.cloned.1.call-update
  689.8 77.8 %reduce-scatter.2.cloned.1.call-done = bf16[128,7168]{1,0:T(8,128)(2,1)} async-done(((bf16[512,7168]{1,0:T(8,128)(2,1)}), bf16[128,7168]{1,0:T(8,128)(2,1)}) %reduce-scatter.2.cloned.1.call-update) | async-done | bytes 1835024 | tf_op jit(solution)/shard_map/reduce_scatter | solution.py:100
  767.6 4.2 add_convert_fusion
  771.8 0.0 copy-done.1
  (2 shorter events, 0.0 us)
Async XLA Ops:
  6.5 54.8 %copy-start = (bf16[16,512,128]{2,1,0:T(8,128)(2,1)S(1)}, bf16[16,512,128]{2,1,0:T(8,128)(2,1)}, u32[]{:S(2)}) copy-start(bf16[16,512,128]{2,1,0:T(8,128)(2,1)} %param.17) | copy-start | bytes 6291460
  6.5 358.1 %all-gather.15.cloned.1.call-start = ((), (), s32[]{:S(2)}) async-start(), calls=%async_computation.6 | async-start | bytes 36700160 | tf_op jit(solution)/shard_map/all_gather | solution.py:6
  6.5 12.5 %collective-permute-start = (bf16[512,512]{1,0:T(8,128)(2,1)}, bf16[512,512]{1,0:T(8,128)(2,1)}, u32[]{:S(2)}, u32[]{:S(2)}) collective-permute-start(bf16[512,512]{1,0:T(8,128)(2,1)} %param.14), channel_id=1, source_target_pairs={{0,4},{4,8},{8,12},{12,16},{16,20},{20,24},{24,28},{28,0},{1,5},{5... | collective-permute-start | bytes 1572872 | tf_op jit(solution)/shard_map/ppermute | solution.py:11
  7.0 11.8 %collective-permute-start.1 = (bf16[256,128]{1,0:T(8,128)(2,1)}, bf16[256,128]{1,0:T(8,128)(2,1)S(1)}, u32[]{:S(2)}, u32[]{:S(2)}) collective-permute-start(bf16[256,128]{1,0:T(8,128)(2,1)} %param.15), channel_id=1, source_target_pairs={{0,4},{4,8},{8,12},{12,16},{16,20},{20,24},{24,28},{28,0},{1,5},{5... | collective-permute-start | bytes 196616 | tf_op jit(solution)/shard_map/ppermute | solution.py:11
  102.2 343.2 %all-gather.7.cloned.1.call-start = ((), (), s32[]{:S(2)}) async-start(), calls=%async_computation.1 | async-start | bytes 9175040 | tf_op jit(solution)/shard_map/all_gather | solution.py:88
  103.0 417.5 %all-gather.9.cloned.1.call-start = ((), (), s32[]{:S(2)}) async-start(), calls=%async_computation.2 | async-start | bytes 8257536 | tf_op jit(solution)/shard_map/all_gather | solution.py:93
  103.7 490.3 %all-gather.11.cloned.1.call-start = ((), (), s32[]{:S(2)}) async-start(), calls=%async_computation.3 | async-start | bytes 8257536 | tf_op jit(solution)/shard_map/all_gather | solution.py:94
  104.3 563.3 %all-gather.13.cloned.1.call-start = ((), (), s32[]{:S(2)}) async-start(), calls=%async_computation.4 | async-start | bytes 8257536 | tf_op jit(solution)/shard_map/all_gather | solution.py:95
  104.9 662.7 %reduce-scatter.2.cloned.1.call-start = ((), (), s32[]{:S(2)}) async-start(), calls=%async_computation.5 | async-start | bytes 9175040 | tf_op jit(solution)/shard_map/reduce_scatter | solution.py:100
  380.8 139.7 %copy-start.2 = (f32[7168]{0:T(1024)S(1)}, f32[7168]{0:T(1024)}, u32[]{:S(2)}) copy-start(f32[7168]{0:T(1024)} %param.20) | copy-start | bytes 86020
  689.8 82.0 %copy-start.1 = (bf16[16,512,128]{2,1,0:T(8,128)(2,1)S(1)}, bf16[16,512,128]{2,1,0:T(8,128)(2,1)}, u32[]{:S(2)}) copy-start(bf16[16,512,128]{2,1,0:T(8,128)(2,1)} %param.17) | copy-start | bytes 6291460
Sparse Core Ops, SparseCore 0:
  102.3 262.2 all-gather.14
  366.5 78.8 all-gather.6
  447.0 73.3 all-gather.8
  522.0 71.9 all-gather.10
  595.5 71.9 all-gather.12
  690.0 77.5 reduce-scatter.1
